TPU v7x, 32 devices: a whole 2x2x4 slice. The times are simulated.
32 devices in a mesh: dev: 32 (over z, y, x, core).
Axes of the slice: x: 2, y: 2, z: 4, core: 2. Of those that a mesh axis runs over, the one named last changes fastest.
Arguments:
- start: float32 [8, 65536], P(None, 'dev'), may hold values from -18 to 18
- self_blocks: bfloat16 [256, 256, 256], P('dev'), may hold values from -1 to 5, as said below
- near_pairs: int32 [2, 3072], P(None, 'dev'), may hold values from 0 to 255, as said below
- near_blocks: bfloat16 [3072, 256, 256], P('dev'), may hold values from -0.08984375 to 0.08984375
- far_pairs: int32 [2, 4096], P(None, 'dev'), may hold values from 0 to 255, as said below
- far_left: bfloat16 [4096, 16, 256], P('dev'), may hold values from -0.375 to 0.375
- far_right: bfloat16 [4096, 16, 256], P('dev'), may hold values from -0.375 to 0.375
Outputs:
- next_basis: float32 [8, 65536], P(None, 'dev')
- hessenberg: float32 [5, 8], replicated
Inputs may be any that keep to these rules, and one draw needn't show every extreme that they name: `self_blocks`: each block equals its transpose. `near_pairs`: the first cluster of a pair lies on the owning device; the second differs from it and lies on the owning device or on the device just before or after it. `far_pairs`: the first cluster of a pair lies on the owning device; the second lies on another device; among one device's 128 pairs at most 8 have their second cluster on any one device, and exactly 8 on the next device and on the device half the axis away.
All inputs are finite; a program needn't handle non-finite values.
Results may differ from a plain program's by a relative error of at most 0.009.
Values may be sent and summed in bfloat16 or wider, within the bound.
A program may use at most 128 MiB of HBM per device.

v0:
```python
import jax
import jax.numpy as jnp
from jax import lax
from jax.sharding import PartitionSpec as P

epsilon = 1e-06


def padded(x, sides, width):
    for axis, dim in sides:
        peers, length = (lax.axis_size(axis), x.shape[dim])
        up = [(i, (i + 1) % peers) for i in range(peers - 1)]
        down = [(j, i) for i, j in up]
        last = lax.slice_in_dim(x, length - width, length, axis=dim)
        leading = lax.slice_in_dim(x, 0, width, axis=dim)
        before = lax.ppermute(last, axis, up)
        after = lax.ppermute(leading, axis, down)
        x = jnp.concatenate([before, x, after], axis=dim)
    return x


def from_behind(value, axis, steps):
    count = lax.axis_size(axis)
    leading, last = (max(0, -steps), min(count, count - steps))
    return lax.ppermute(value, axis, [(source, source + steps) for source in range(leading, last)])


def add_by_cluster(labels, terms, groups):
    onehot = (labels[:, None] == jnp.arange(groups, dtype=jnp.int32)[None, :]).astype(jnp.float32)
    return jnp.einsum("pc,pm->cm", onehot, terms, precision=lax.Precision.HIGHEST)


def far_layout(far_pairs, cluster_count):
    devices = lax.axis_size("dev")
    position = lax.axis_index("dev")
    far_count = far_pairs.shape[1]
    most = max(2, 2 * far_count // devices)
    row_local = far_pairs[0] - position * cluster_count
    target = far_pairs[1] // cluster_count
    col_local = far_pairs[1] % cluster_count
    hits = (target[:, None] == jnp.arange(devices, dtype=jnp.int32)[None, :]).astype(jnp.int32)
    place = jnp.sum((jnp.cumsum(hits, axis=0) - 1) * hits, axis=1)
    slot = target * most + place
    return (row_local, col_local, slot, most)


def apply_operator(narrow, self_blocks, near_pairs, near_blocks, far_pairs, far_left, far_right):
    rhs_count, width = narrow.shape
    panel_count = self_blocks.shape[1]
    cluster_count = width // panel_count
    devices = lax.axis_size("dev")
    position = lax.axis_index("dev")
    flat_width = rhs_count * panel_count
    local = narrow.reshape(rhs_count, cluster_count, panel_count).transpose(1, 0, 2)
    total = jnp.einsum("crb,cab->cra", local, self_blocks, preferred_element_type=jnp.float32)
    total = total.reshape(cluster_count, flat_width)
    extended = padded(narrow, (("dev", 1),), width)
    extended = extended.reshape(rhs_count, 3 * cluster_count, panel_count).transpose(1, 0, 2)
    near_rows = near_pairs[0] - position * cluster_count + cluster_count
    near_cols = near_pairs[1] - (position - 1) * cluster_count
    pair_count = near_blocks.shape[0]
    to_rows = jnp.einsum(
        "prb,pab->pra", extended[near_cols], near_blocks, preferred_element_type=jnp.float32
    )
    to_cols = jnp.einsum(
        "pra,pab->prb", extended[near_rows], near_blocks, preferred_element_type=jnp.float32
    )
    gathered = add_by_cluster(near_rows, to_rows.reshape(pair_count, flat_width), 3 * cluster_count)
    gathered = gathered + add_by_cluster(
        near_cols, to_cols.reshape(pair_count, flat_width), 3 * cluster_count
    )
    from_after = from_behind(gathered[:cluster_count].astype(jnp.bfloat16), "dev", -1).astype(
        jnp.float32
    )
    from_before = from_behind(gathered[2 * cluster_count :].astype(jnp.bfloat16), "dev", 1).astype(
        jnp.float32
    )
    total = total + gathered[cluster_count : 2 * cluster_count] + from_after + from_before
    far_count = far_pairs.shape[1]
    row_local, col_local, slot, most = far_layout(far_pairs, cluster_count)
    lean = jnp.einsum(
        "pka,pra->pkr", far_left, local[row_local], preferred_element_type=jnp.float32
    ).astype(jnp.bfloat16)
    request = jnp.zeros((devices * most,), jnp.int32).at[slot].set(col_local).reshape(devices, most)
    served_ids = lax.all_to_all(request, "dev", split_axis=0, concat_axis=0, tiled=True).reshape(
        devices * most
    )
    served = local[served_ids].reshape(devices, most, flat_width)
    arrived = lax.all_to_all(served, "dev", split_axis=0, concat_axis=0, tiled=True).reshape(
        devices * most, rhs_count, panel_count
    )
    coeff = jnp.einsum(
        "pkb,prb->pkr", far_right, arrived[slot], preferred_element_type=jnp.float32
    ).astype(jnp.bfloat16)
    outgoing = jnp.einsum("pkb,pkr->prb", far_right, lean, preferred_element_type=jnp.float32)
    outbox = (
        jnp.zeros((devices * most, flat_width), jnp.float32)
        .at[slot]
        .set(outgoing.reshape(far_count, flat_width))
    )
    col_terms = lax.all_to_all(
        outbox.reshape(devices, most, flat_width), "dev", split_axis=0, concat_axis=0, tiled=True
    ).reshape(devices * most, flat_width)
    row_terms = jnp.einsum("pka,pkr->pra", far_left, coeff, preferred_element_type=jnp.float32)
    total = total + add_by_cluster(
        row_local, row_terms.reshape(far_count, flat_width), cluster_count
    )
    total = total + add_by_cluster(served_ids, col_terms, cluster_count)
    return (
        total.reshape(cluster_count, rhs_count, panel_count)
        .transpose(1, 0, 2)
        .reshape(rhs_count, width)
    )


def orthogonalize(basis, image, count):
    heights = []
    remainder = image
    for vector in basis:
        height = lax.psum(jnp.sum(vector * remainder, axis=1), "dev") / count
        remainder = remainder - height[:, None] * vector
        heights.append(height)
    mean_square = lax.psum(jnp.sum(remainder * remainder, axis=1), "dev") / count
    norm_value = jnp.sqrt(mean_square + epsilon)
    return (heights, remainder / norm_value[:, None], norm_value)


def per_device(start, self_blocks, near_pairs, near_blocks, far_pairs, far_left, far_right):
    count = float(start.shape[1] * lax.axis_size("dev"))
    scale = jnp.sqrt(lax.psum(jnp.sum(start * start, axis=1), "dev") / count + epsilon)
    basis = [start / scale[:, None]]
    entries = []
    for iteration in range(2):
        image = apply_operator(
            basis[-1].astype(jnp.bfloat16),
            self_blocks,
            near_pairs,
            near_blocks,
            far_pairs,
            far_left,
            far_right,
        )
        heights, following, norm_value = orthogonalize(basis, image, count)
        entries.extend(heights)
        entries.append(norm_value)
        basis.append(following)
    return (basis[-1], jnp.stack(entries))


def solution(mesh):
    in_specs = (
        P(None, "dev"),
        P("dev", None, None),
        P(None, "dev"),
        P("dev", None, None),
        P(None, "dev"),
        P("dev", None, None),
        P("dev", None, None),
    )
    out_specs = (P(None, "dev"), P())
    return jax.shard_map(
        per_device, mesh=mesh, in_specs=in_specs, out_specs=out_specs, check_vma=False
    )
```

profile of v0, /device:TPU:0, one launch (start us, length us, event | category | flops | bytes accessed | tf_op | source)
XLA Modules:
  0.0 465.6 jit_solution(5517014162932813548)
XLA Ops:
  6.0 7.3 %all-to-all-start = ((s32[32,1,8]{2,1,0:T(1,128)}), s32[32,1,8]{2,1,0:T(1,128)S(1)}, u32[]{:S(2)}, u32[]{:S(2)}) async-start(s32[32,1,8]{2,1,0:T(1,128)} %bitcast.18), calls=%async_computation | async-start | bytes 32768 | tf_op jit(solution)/shard_map/all_to_all | solution.py:85
  13.3 40.5 %psum.42 = f32[8]{0:T(128)S(1)} all-reduce(f32[8]{0:T(128)S(1)} %multiply_reduce_fusion.5), channel_id=1, replica_groups=mesh['dev'=32] {'dev'}, use_global_device_ids=true, to_apply=%region_1.0 | all-reduce | flops 8 | bytes 64 | tf_op jit(solution)/shard_map/psum | solution.py:130
  56.8 1.3 reshape.319
  58.2 4.6 all-to-all-start.1
  62.8 2.1 collective-permute-start
  64.9 1.3 collective-permute-start.1
  66.2 1.4 gather_fusion.4
  67.6 1.6 fusion.5
  69.2 1.3 copy.15
  70.5 3.4 scatter_custom_fusion.1
  74.3 14.7 %all-to-all-done.1 = bf16[32,8,2048]{2,1,0:T(8,128)(2,1)} async-done(((bf16[32,8,2048]{2,1,0:T(8,128)(2,1)}), bf16[32,8,2048]{2,1,0:T(8,128)(2,1)}, u32[]{:S(2)}, u32[]{:S(2)}) %all-to-all-start.1) | async-done | bytes 1048608 | tf_op jit(solution)/shard_map/all_to_all | solution.py:89
  89.0 3.8 all-to-all-start.2
  94.2 7.9 %fusion.54 = f32[96,8,256]{2,1,0:T(8,128)S(1)} fusion(bf16[96,8,256]{2,1,0:T(8,128)(2,1)S(1)} %gather_fusion, bf16[96,256,256]{2,1,0:T(8,128)(2,1)} %param.10), kind=kOutput, calls=%fused_computation.127 | convolution fusion | flops 100663296 | bytes 13762560 | tf_op jit(solution)/shard_map/prb,pab->pra/dot_general | solution.py:62
  103.0 6.3 %fusion.55 = f32[96,8,256]{2,1,0:T(8,128)S(1)} fusion(bf16[96,8,256]{2,1,0:T(8,128)(2,1)S(1)} %gather_fusion.1, bf16[96,256,256]{2,1,0:T(8,128)(2,1)} %param.10), kind=kOutput, calls=%fused_computation.128 | convolution fusion | flops 100663296 | bytes 13762560 | tf_op jit(solution)/shard_map/pra,pab->prb/dot_general | solution.py:65
  111.1 1.3 collective-permute-start.2
  112.4 3.2 collective-permute-start.3
  115.6 1.5 copy.13
  117.1 1.5 gather_fusion.3
  118.6 1.6 fusion.4
  120.2 1.3 copy.14
  121.5 20.2 %all-to-all-done.2 = f32[32,8,2048]{2,1,0:T(8,128)} async-done(((f32[32,8,2048]{2,1,0:T(8,128)}), f32[32,8,2048]{2,1,0:T(8,128)}, u32[]{:S(2)}, u32[]{:S(2)}) %all-to-all-start.2) | async-done | bytes 2097184 | tf_op jit(solution)/shard_map/all_to_all | solution.py:101
  141.7 2.4 fusion.2
  145.4 38.1 %psum.43 = f32[8]{0:T(128)S(1)} all-reduce(f32[8]{0:T(128)S(1)} %multiply_reduce_fusion.4), channel_id=1, replica_groups=mesh['dev'=32] {'dev'}, use_global_device_ids=true, to_apply=%region_7.8 | all-reduce | flops 8 | bytes 64 | tf_op jit(solution)/shard_map/psum | solution.py:120
  184.3 41.0 %psum.44 = f32[8]{0:T(128)S(1)} all-reduce(f32[8]{0:T(128)S(1)} %multiply_reduce_fusion.3), channel_id=1, replica_groups=mesh['dev'=32] {'dev'}, use_global_device_ids=true, to_apply=%region_9.10 | all-reduce | flops 8 | bytes 64 | tf_op jit(solution)/shard_map/psum | solution.py:123
  226.8 1.3 reshape.332
  228.1 5.1 %all-to-all-start.3 = ((bf16[32,8,2048]{2,1,0:T(8,128)(2,1)}), bf16[32,8,2048]{2,1,0:T(8,128)(2,1)}, u32[]{:S(2)}, u32[]{:S(2)}) async-start(bf16[32,8,2048]{2,1,0:T(8,128)(2,1)} %reshape.332), calls=%async_computation.3 | async-start | bytes 2097152 | tf_op jit(solution)/shard_map/all_to_all | solution.py:89
  233.3 1.5 gather_fusion.9
  234.8 1.6 fusion.7
  236.4 1.3 copy.22
  237.7 3.3 scatter_custom_fusion.2
  241.0 18.5 %all-to-all-done.3 = bf16[32,8,2048]{2,1,0:T(8,128)(2,1)} async-done(((bf16[32,8,2048]{2,1,0:T(8,128)(2,1)}), bf16[32,8,2048]{2,1,0:T(8,128)(2,1)}, u32[]{:S(2)}, u32[]{:S(2)}) %all-to-all-start.3) | async-done | bytes 1048608 | tf_op jit(solution)/shard_map/all_to_all | solution.py:89
  259.5 3.7 all-to-all-start.4
  263.2 2.1 collective-permute-start.4
  265.3 1.3 collective-permute-start.5
  267.7 1.9 collective-permute-done.5
  270.3 1.5 gather_fusion.6
  271.8 8.0 %fusion.56 = f32[96,8,256]{2,1,0:T(8,128)S(1)} fusion(bf16[96,8,256]{2,1,0:T(8,128)(2,1)S(1)} %gather_fusion.5, bf16[96,256,256]{2,1,0:T(8,128)(2,1)} %param.10), kind=kOutput, calls=%fused_computation.129 | convolution fusion | flops 100663296 | bytes 13762560 | tf_op jit(solution)/shard_map/prb,pab->pra/dot_general | solution.py:62
  280.1 6.3 %fusion.57 = f32[96,8,256]{2,1,0:T(8,128)S(1)} fusion(bf16[96,8,256]{2,1,0:T(8,128)(2,1)S(1)} %copy-done.6, bf16[96,256,256]{2,1,0:T(8,128)(2,1)} %param.10), kind=kOutput, calls=%fused_computation.130 | convolution fusion | flops 100663296 | bytes 13762560 | tf_op jit(solution)/shard_map/pra,pab->prb/dot_general | solution.py:65
  288.2 1.3 collective-permute-start.6
  289.5 12.6 %collective-permute-start.7 = (bf16[8,2048]{1,0:T(8,128)(2,1)}, bf16[8,2048]{1,0:T(8,128)(2,1)S(1)}, u32[]{:S(2)}, u32[]{:S(2)}) collective-permute-start(bf16[8,2048]{1,0:T(8,128)(2,1)} %get-tuple-element.9), channel_id=1, source_target_pairs={{0,1},{1,2},{2,3},{3,4},{4,5},{5,6},{6,7},{7,8},{8,9},{9,10},{10,1... | collective-permute-start | bytes 98312 | tf_op jit(solution)/shard_map/ppermute | solution.py:25
  302.1 1.5 copy.20
  303.6 1.5 gather_fusion.8
  305.1 1.6 fusion.6
  307.6 4.5 all-to-all-done.4
  312.1 2.4 fusion.15
  314.7 69.0 %psum.45 = f32[8]{0:T(128)S(1)} all-reduce(f32[8]{0:T(128)S(1)} %multiply_reduce_fusion.2), channel_id=1, replica_groups=mesh['dev'=32] {'dev'}, use_global_device_ids=true, to_apply=%region_12.13 | all-reduce | flops 8 | bytes 64 | tf_op jit(solution)/shard_map/psum | solution.py:120
  383.9 39.9 %psum.46 = f32[8]{0:T(128)S(1)} all-reduce(f32[8]{0:T(128)S(1)} %multiply_reduce_fusion.1), channel_id=1, replica_groups=mesh['dev'=32] {'dev'}, use_global_device_ids=true, to_apply=%region_14.15 | all-reduce | flops 8 | bytes 64 | tf_op jit(solution)/shard_map/psum | solution.py:120
  424.1 40.2 %psum.47 = f32[8]{0:T(128)S(1)} all-reduce(f32[8]{0:T(128)S(1)} %get-tuple-element.2), channel_id=1, replica_groups=mesh['dev'=32] {'dev'}, use_global_device_ids=true, to_apply=%region_16.17 | all-reduce | flops 8 | bytes 64 | tf_op jit(solution)/shard_map/psum | solution.py:123
  (112 shorter events, 22.8 us)
Async XLA Ops:
  0.6 67.0 %copy-start = (bf16[128,16,256]{2,1,0:T(8,128)(2,1)S(1)}, bf16[128,16,256]{2,1,0:T(8,128)(2,1)}, u32[]{:S(2)}) copy-start(bf16[128,16,256]{2,1,0:T(8,128)(2,1)} %param.13) | copy-start | bytes 3145732
  4.3 89.1 %copy-start.17 = (s32[128]{0:T(128)}, s32[128]{0:T(128)S(1)}, u32[]{:S(2)}) copy-start(s32[128]{0:T(128)S(1)} %get-tuple-element.17) | copy-start | bytes 1540
  6.0 48.8 %all-to-all-start = ((s32[32,1,8]{2,1,0:T(1,128)}), s32[32,1,8]{2,1,0:T(1,128)S(1)}, u32[]{:S(2)}, u32[]{:S(2)}) async-start(s32[32,1,8]{2,1,0:T(1,128)} %bitcast.18), calls=%async_computation | async-start | bytes 32768 | tf_op jit(solution)/shard_map/all_to_all | solution.py:85
  58.2 9.5 %copy-start.1 = (bf16[128,16,256]{2,1,0:T(8,128)(2,1)S(1)}, bf16[128,16,256]{2,1,0:T(8,128)(2,1)}, u32[]{:S(2)}) copy-start(bf16[128,16,256]{2,1,0:T(8,128)(2,1)} %param.12) | copy-start | bytes 3145732
  58.2 30.8 %all-to-all-start.1 = ((bf16[32,8,2048]{2,1,0:T(8,128)(2,1)}), bf16[32,8,2048]{2,1,0:T(8,128)(2,1)}, u32[]{:S(2)}, u32[]{:S(2)}) async-start(bf16[32,8,2048]{2,1,0:T(8,128)(2,1)} %reshape.319), calls=%async_computation.1 | async-start | bytes 2097152 | tf_op jit(solution)/shard_map/all_to_all | solution.py:89
  62.8 30.7 %collective-permute-start = (bf16[8,2048]{1,0:T(8,128)(2,1)S(1)}, bf16[8,2048]{1,0:T(8,128)(2,1)S(1)}, u32[]{:S(2)}, u32[]{:S(2)}) collective-permute-start(bf16[8,2048]{1,0:T(8,128)(2,1)S(1)} %fusion.48), channel_id=1, source_target_pairs={{0,1},{1,2},{2,3},{3,4},{4,5},{5,6},{6,7},{7,8},{8,9},{9,10},{10,1... | collective-permute-start | bytes 98312 | tf_op jit(solution)/shard_map/ppermute | solution.py:16
  64.9 28.7 %collective-permute-start.1 = (bf16[8,2048]{1,0:T(8,128)(2,1)S(1)}, bf16[8,2048]{1,0:T(8,128)(2,1)S(1)}, u32[]{:S(2)}, u32[]{:S(2)}) collective-permute-start(bf16[8,2048]{1,0:T(8,128)(2,1)S(1)} %fusion.48), channel_id=1, source_target_pairs={{1,0},{2,1},{3,2},{4,3},{5,4},{6,5},{7,6},{8,7},{9,8},{10,9},{11,1... | collective-permute-start | bytes 98312 | tf_op jit(solution)/shard_map/ppermute | solution.py:17
  66.2 3.0 copy-start.8
  70.5 3.4 copy-start.3
  70.5 3.8 copy-start.15
  89.0 3.8 copy-start.18
  89.0 52.7 %all-to-all-start.2 = ((f32[32,8,2048]{2,1,0:T(8,128)}), f32[32,8,2048]{2,1,0:T(8,128)}, u32[]{:S(2)}, u32[]{:S(2)}) async-start(f32[32,8,2048]{2,1,0:T(8,128)} %bitcast.158), calls=%async_computation.2 | async-start | bytes 4194304 | tf_op jit(solution)/shard_map/all_to_all | solution.py:101
  92.8 9.3 %copy-start.10 = (s32[1024]{0:T(1024)}, s32[1024]{0:T(1024)S(1)}, u32[]{:S(2)}) copy-start(s32[1024]{0:T(1024)S(1)} %get-tuple-element.33) | copy-start | bytes 12292
  92.8 9.5 %copy-start.9 = (s32[1024]{0:T(1024)}, s32[1024]{0:T(1024)S(1)}, u32[]{:S(2)}) copy-start(s32[1024]{0:T(1024)S(1)} %get-tuple-element.32) | copy-start | bytes 12292
  93.4 16.2 %copy-start.11 = (s32[96]{0:T(128)}, s32[96]{0:T(128)S(1)}, u32[]{:S(2)}) copy-start(s32[96]{0:T(128)S(1)} %get-tuple-element.13) | copy-start | bytes 1156
  93.4 16.6 %copy-start.13 = (s32[96]{0:T(128)}, s32[96]{0:T(128)S(1)}, u32[]{:S(2)}) copy-start(s32[96]{0:T(128)S(1)} %get-tuple-element.12) | copy-start | bytes 1156
  111.1 33.0 %collective-permute-start.2 = (bf16[8,2048]{1,0:T(8,128)(2,1)}, bf16[8,2048]{1,0:T(8,128)(2,1)S(1)}, u32[]{:S(2)}, u32[]{:S(2)}) collective-permute-start(bf16[8,2048]{1,0:T(8,128)(2,1)} %get-tuple-element.10), channel_id=1, source_target_pairs={{1,0},{2,1},{3,2},{4,3},{5,4},{6,5},{7,6},{8,7},{9,8},{10,9},{11,1... | collective-permute-start | bytes 98312 | tf_op jit(solution)/shard_map/ppermute | solution.py:25
  112.4 31.7 %collective-permute-start.3 = (bf16[8,2048]{1,0:T(8,128)(2,1)}, bf16[8,2048]{1,0:T(8,128)(2,1)S(1)}, u32[]{:S(2)}, u32[]{:S(2)}) collective-permute-start(bf16[8,2048]{1,0:T(8,128)(2,1)} %get-tuple-element.11), channel_id=1, source_target_pairs={{0,1},{1,2},{2,3},{3,4},{4,5},{5,6},{6,7},{7,8},{8,9},{9,10},{10,1... | collective-permute-start | bytes 98312 | tf_op jit(solution)/shard_map/ppermute | solution.py:25
  121.5 22.6 %copy-start.5 = (f32[16,8,8,256]{3,1,2,0:T(8,128)S(1)}, f32[16,8,8,256]{3,1,2,0:T(8,128)}, u32[]{:S(2)}) copy-start(f32[16,8,8,256]{3,1,2,0:T(8,128)} %copy.14) | copy-start | bytes 3145732
  121.5 23.7 %copy-start.2 = (f32[8,2048]{1,0:T(8,128)S(1)}, f32[8,2048]{1,0:T(8,128)}, u32[]{:S(2)}) copy-start(f32[8,2048]{1,0:T(8,128)} %param.7) | copy-start | bytes 196612
  228.1 31.3 %all-to-all-start.3 = ((bf16[32,8,2048]{2,1,0:T(8,128)(2,1)}), bf16[32,8,2048]{2,1,0:T(8,128)(2,1)}, u32[]{:S(2)}, u32[]{:S(2)}) async-start(bf16[32,8,2048]{2,1,0:T(8,128)(2,1)} %reshape.332), calls=%async_computation.3 | async-start | bytes 2097152 | tf_op jit(solution)/shard_map/all_to_all | solution.py:89
  259.5 7.2 %copy-start.4 = (bf16[8,256,256]{2,1,0:T(8,128)(2,1)S(1)}, bf16[8,256,256]{2,1,0:T(8,128)(2,1)}, u32[]{:S(2)}) copy-start(bf16[8,256,256]{2,1,0:T(8,128)(2,1)} %param.8) | copy-start | bytes 3145732
  259.5 52.6 %all-to-all-start.4 = ((f32[32,8,2048]{2,1,0:T(8,128)}), f32[32,8,2048]{2,1,0:T(8,128)}, u32[]{:S(2)}, u32[]{:S(2)}) async-start(f32[32,8,2048]{2,1,0:T(8,128)} %bitcast.157), calls=%async_computation.4 | async-start | bytes 4194304 | tf_op jit(solution)/shard_map/all_to_all | solution.py:101
  263.2 4.4 collective-permute-start.4
  265.3 4.2 collective-permute-start.5
  271.8 8.2 %copy-start.6 = (bf16[96,8,256]{2,1,0:T(8,128)(2,1)S(1)}, bf16[96,8,256]{2,1,0:T(8,128)(2,1)}, u32[]{:S(2)}) copy-start(bf16[96,8,256]{2,1,0:T(8,128)(2,1)} %gather_fusion.6) | copy-start | bytes 1179652
  280.1 6.6 %copy-start.12 = (s32[96]{0:T(128)S(1)}, s32[96]{0:T(128)}, u32[]{:S(2)}) copy-start(s32[96]{0:T(128)} %copy-done.11) | copy-start | bytes 1156
  286.4 0.7 copy-start.14
  288.2 19.4 %collective-permute-start.6 = (bf16[8,2048]{1,0:T(8,128)(2,1)}, bf16[8,2048]{1,0:T(8,128)(2,1)S(1)}, u32[]{:S(2)}, u32[]{:S(2)}) collective-permute-start(bf16[8,2048]{1,0:T(8,128)(2,1)} %get-tuple-element.8), channel_id=1, source_target_pairs={{1,0},{2,1},{3,2},{4,3},{5,4},{6,5},{7,6},{8,7},{9,8},{10,9},{11,1... | collective-permute-start | bytes 98312 | tf_op jit(solution)/shard_map/ppermute | solution.py:25
  289.5 18.1 %collective-permute-start.7 = (bf16[8,2048]{1,0:T(8,128)(2,1)}, bf16[8,2048]{1,0:T(8,128)(2,1)S(1)}, u32[]{:S(2)}, u32[]{:S(2)}) collective-permute-start(bf16[8,2048]{1,0:T(8,128)(2,1)} %get-tuple-element.9), channel_id=1, source_target_pairs={{0,1},{1,2},{2,3},{3,4},{4,5},{5,6},{6,7},{7,8},{8,9},{9,10},{10,1... | collective-permute-start | bytes 98312 | tf_op jit(solution)/shard_map/ppermute | solution.py:25
  305.1 1.9 copy-start.16
  306.7 5.4 %copy-start.7 = (f32[1,8,8,256]{3,1,2,0:T(8,128)S(1)}, f32[1,8,8,256]{3,1,2,0:T(8,128)}, u32[]{:S(2)}) copy-start(f32[1,8,8,256]{3,1,2,0:T(8,128)} %copy.17) | copy-start | bytes 196612
  307.0 157.9 %copy-start.19 = (f32[1,8]{1,0:T(1,128)S(1)}, f32[1,8]{1,0:T(1,128)}, u32[]{:S(2)}) copy-start(f32[1,8]{1,0:T(1,128)} %get-tuple-element.26) | copy-start | bytes 100
  307.1 157.9 %copy-start.20 = (f32[1,8]{1,0:T(1,128)S(1)}, f32[1,8]{1,0:T(1,128)}, u32[]{:S(2)}) copy-start(f32[1,8]{1,0:T(1,128)} %get-tuple-element.24) | copy-start | bytes 100
where the time goes:
time: 467 us; the launch traced here: 466 us
  blocking collectives  269 us (58%)
  waiting for transfers between devices  59.7 us (13%)
  starting transfers between devices  49.7 us (11%)
  matrix products  43.6 us (9%)
  local copies, waits for them, and re-layouts  33.7 us (7%)
  other arithmetic  8.8 us (2%)
    psum x3, blocking collectives, orthogonalize(): height = lax.psum(jnp.sum(vector * remainder, axis=1), 'dev') / count  147 us
    psum x2, blocking collectives, orthogonalize(): lax.psum(jnp.sum(remainder * remainder, axis=1), 'dev') / count  81.2 us
    psum x1, blocking collectives, per_device(): lax.psum(jnp.sum(start * start, axis=1), 'dev') / count + epsilon  40.5 us
    all_to_all x2, waiting for transfers between devices, apply_operator(): lax.all_to_all(served, 'dev', split_axis=0, concat_axis=0, tiled=True)  33.1 us
    all_to_all x2, waiting for transfers between devices, apply_operator(): lax.all_to_all(outbox.reshape(devices, most, flat_width), 'dev', split_ax...  24.7 us
    ppermute x4, starting transfers between devices, from_behind(): lax.ppermute(value, axis, [(source, source + steps) for source in range(l...  18.4 us
    dot_general x2, matrix products, apply_operator(): jnp.einsum('prb,pab->pra', extended[near_cols], near_blocks, preferred_el...  15.9 us
    dot_general x2, matrix products, apply_operator(): jnp.einsum('pra,pab->prb', extended[near_rows], near_blocks, preferred_el...  12.6 us
  transfers between devices with their start and end apart: 13, of which 5 were waited for; matrix products, arithmetic and copies ran while one was open for 15% of the time, Pallas kernels for 0%

commit v1 on v0

v1 whole, which is shorter than its diff:
```python
import functools
import jax
import jax.numpy as jnp
from jax import lax
from jax.experimental import pallas as pl
from jax.experimental.pallas import tpu as pltpu
from jax.sharding import PartitionSpec as P

epsilon = 1e-06
LANES = 128
MESH = pl.DeviceIdType.MESH
F32 = jnp.float32
BF16 = jnp.bfloat16
NEAR_CHUNKS = 4
REDUCTIONS = 5


def dot_nn(a, b):
    return lax.dot_general(a, b, (((1,), (0,)), ((), ())), preferred_element_type=F32)


def dot_nt(a, b):
    return lax.dot_general(a, b, (((1,), (1,)), ((), ())), preferred_element_type=F32)


def row_sum(a):
    return jnp.sum(jnp.sum(a, axis=0), axis=1, keepdims=True)


def one_hot_sum(keys, terms, groups):
    count = terms.shape[0]
    hot = jnp.where(lax.broadcasted_iota(jnp.int32, (groups, count), 0) == keys, 1.0, 0.0).astype(BF16)
    high = terms.astype(BF16)
    low = (terms - high.astype(F32)).astype(BF16)
    return dot_nn(hot, high) + dot_nn(hot, low)


def kernel(
    n, most, total_count,
    near_ids, perm, start_ref, keys_ref, row_ids, col_ids, self_hbm, near_hbm, left_hbm, right_hbm,
    out_ref, hess_ref,
    selfs, nears, lefts, rights, factors, outgoing, id_recv, stat_send, stat_recv,
    halo_send, halo_recv, part_send, part_recv, message, message_recv,
    extended, terms, basis,
    load_sem, stat_ssem, stat_rsem, fact_ssem, fact_rsem, id_ssem, id_rsem,
    halo_ssem, halo_rsem, part_ssem, part_rsem, msg_ssem, msg_rsem,
):
    me = lax.axis_index("dev")
    after = lax.rem(me + 1, n)
    before = lax.rem(me + n - 1, n)
    clusters, panels, _ = self_hbm.shape
    pairs = near_hbm.shape[0]
    rank = left_hbm.shape[1]
    rhs = start_ref.shape[0]
    used = most * rank
    flat = clusters * rhs

    def peer_loop(body):
        def step(i, carry):
            body(lax.rem(me + i, n))
            return carry
        lax.fori_loop(1, n, step, 0)

    def remote(src, dst, ssem, rsem, peer):
        return pltpu.make_async_remote_copy(
            src_ref=src, dst_ref=dst, send_sem=ssem, recv_sem=rsem,
            device_id=(peer,), device_id_type=MESH,
        )

    def wait_bytes(ref, sem):
        pltpu.make_async_copy(ref, ref, sem).wait()

    right_copy = pltpu.make_async_copy(right_hbm, rights, load_sem.at[0])
    right_copy.start()
    left_copy = pltpu.make_async_copy(left_hbm, lefts, load_sem.at[1])
    left_copy.start()
    loads = [pltpu.make_async_copy(self_hbm, selfs, load_sem.at[2])]
    size = pairs // NEAR_CHUNKS
    for part in range(NEAR_CHUNKS):
        span = pl.ds(part * size, size)
        loads.append(pltpu.make_async_copy(near_hbm.at[span], nears.at[span], load_sem.at[3 + part]))
    for load in loads:
        load.start()

    barrier = pltpu.get_barrier_semaphore()
    peer_loop(lambda peer: pl.semaphore_signal(barrier, inc=1, device_id=(peer,), device_id_type=MESH))

    lane = lax.broadcasted_iota(jnp.int32, (rhs, LANES), 1)

    def send_stats(index, values):
        block = jnp.zeros((rhs, LANES), F32)
        for place, value in enumerate(values):
            block = jnp.where(lane == place, value, block)
        stat_send[index] = block
        stat_recv[index, me] = block
        peer_loop(lambda peer: remote(
            stat_send.at[index], stat_recv.at[index, me], stat_ssem.at[index], stat_rsem.at[index], peer
        ).start())

    def get_stats(index, count):
        wait_bytes(stat_recv.at[index, pl.ds(0, n - 1)], stat_rsem.at[index])
        total = jnp.sum(stat_recv[index], axis=0)
        return [
            jnp.sum(jnp.where(lane == place, total, 0.0), axis=1, keepdims=True) / total_count
            for place in range(count)
        ]

    first = jnp.stack([start_ref[:, c * panels:(c + 1) * panels] for c in range(clusters)], axis=0)
    partial = row_sum(first * first)

    id_recv[me] = jnp.full((rhs, LANES), -1, jnp.int32)
    if used < LANES:
        def clear(t, carry):
            factors[t] = jnp.zeros((2 * LANES, panels), BF16)
            return carry
        lax.fori_loop(0, n, clear, 0)
    else:
        factors[me] = jnp.zeros((2 * LANES, panels), BF16)
    for it in range(2):
        message_recv[it, me] = jnp.zeros((2 * rhs, LANES), BF16)

    pl.semaphore_wait(barrier, n - 1)
    send_stats(0, [partial])

    right_copy.wait()
    left_copy.wait()

    def send_factors(peer):
        for m in range(most):
            pair = perm[peer * most + m]
            outgoing[peer, pl.ds(m * rank, rank)] = rights[pair]
        remote(col_ids.at[peer], id_recv.at[me], id_ssem.at[0], id_rsem.at[0], peer).start()
        remote(
            outgoing.at[peer], factors.at[me, pl.ds(0, used)], fact_ssem.at[0], fact_rsem.at[0], peer
        ).start()
        for m in range(most):
            pair = perm[peer * most + m]
            factors[peer, pl.ds(LANES + m * rank, rank)] = lefts[pair]

    peer_loop(send_factors)

    (square,) = get_stats(0, 1)
    scale = jnp.sqrt(square + epsilon)
    basis[0] = first / scale[None]

    for load in loads:
        load.wait()

    heights = []
    for it in range(2):
        vector = basis[it].reshape(flat, panels).astype(BF16)
        halo_send[it] = vector
        halos = [
            remote(halo_send.at[it], halo_recv.at[it, 0], halo_ssem.at[it, 0], halo_rsem.at[it, 0], after),
            remote(halo_send.at[it], halo_recv.at[it, 1], halo_ssem.at[it, 1], halo_rsem.at[it, 1], before),
        ]
        for halo in halos:
            halo.start()
        extended[pl.ds(clusters, clusters)] = vector.astype(F32).reshape(clusters, rhs, panels)

        def exchange_far():
            if it == 0:
                wait_bytes(factors.at[pl.ds(0, n - 1), pl.ds(0, used)], fact_rsem.at[0])
                wait_bytes(id_recv.at[pl.ds(0, n - 1)], id_rsem.at[0])

            def products(t4, carry):
                for u in range(4):
                    t = t4 * 4 + u
                    e = dot_nt(vector, factors[t])
                    coeff = jnp.zeros((rhs, LANES), F32)
                    lean = jnp.zeros((rhs, LANES), F32)
                    for c in range(clusters):
                        rows = slice(c * rhs, (c + 1) * rhs)
                        coeff = jnp.where(id_recv[t] == c, e[rows, :LANES], coeff)
                        lean = jnp.where(row_ids[t] == c, e[rows, LANES:], lean)
                    message[it, t] = jnp.concatenate([coeff, lean], axis=0).astype(BF16)
                return carry

            lax.fori_loop(0, n // 4, products, 0)
            peer_loop(lambda peer: remote(
                message.at[it, peer], message_recv.at[it, me], msg_ssem.at[it], msg_rsem.at[it], peer
            ).start())

        if it == 1:
            exchange_far()

        def to_cols(p8, carry):
            for u in range(8):
                p = p8 * 8 + u
                x = extended[near_ids[0, p] + clusters].astype(BF16)
                terms[p] = dot_nn(x, nears[p])
            return carry

        lax.fori_loop(0, pairs // 8, to_cols, 0)
        sums = one_hot_sum(keys_ref[1:2, :], terms[...].reshape(pairs * rhs, panels), 3 * flat)
        part_send[it, 0] = sums[:flat].astype(BF16)
        part_send[it, 1] = sums[2 * flat:].astype(BF16)
        shares = [
            remote(part_send.at[it, 0], part_recv.at[it, 0], part_ssem.at[it, 0], part_rsem.at[it, 0], before),
            remote(part_send.at[it, 1], part_recv.at[it, 1], part_ssem.at[it, 1], part_rsem.at[it, 1], after),
        ]
        for share in shares:
            share.start()
        image = sums[flat:2 * flat]
        image = image + jnp.concatenate(
            [dot_nt(vector[c * rhs:(c + 1) * rhs], selfs[c]) for c in range(clusters)], axis=0
        )
        for halo in halos:
            halo.wait_recv()
        extended[pl.ds(0, clusters)] = halo_recv[it, 0].astype(F32).reshape(clusters, rhs, panels)
        extended[pl.ds(2 * clusters, clusters)] = halo_recv[it, 1].astype(F32).reshape(
            clusters, rhs, panels
        )

        def to_rows(p8, carry):
            for u in range(8):
                p = p8 * 8 + u
                x = extended[near_ids[1, p]].astype(BF16)
                terms[p] = dot_nt(x, nears[p])
            return carry

        lax.fori_loop(0, pairs // 8, to_rows, 0)
        image = image + one_hot_sum(keys_ref[0:1, :], terms[...].reshape(pairs * rhs, panels), flat)
        if it == 0:
            exchange_far()
        for share in shares:
            share.wait_recv()
        has_before = jnp.where(me > 0, 1.0, 0.0)
        has_after = jnp.where(me < n - 1, 1.0, 0.0)
        image = image + part_recv[it, 0].astype(F32) * has_after + part_recv[it, 1].astype(F32) * has_before
        wait_bytes(message_recv.at[it, pl.ds(0, n - 1)], msg_rsem.at[it])

        def far_terms(t4, total):
            for u in range(4):
                t = t4 * 4 + u
                arrived = message_recv[it, t].astype(F32)
                coeff, lean = arrived[:rhs], arrived[rhs:]
                spread = jnp.concatenate(
                    [
                        jnp.concatenate(
                            [
                                jnp.where(id_recv[t] == c, lean, 0.0),
                                jnp.where(row_ids[t] == c, coeff, 0.0),
                            ],
                            axis=1,
                        )
                        for c in range(clusters)
                    ],
                    axis=0,
                ).astype(BF16)
                total = total + dot_nn(spread, factors[t])
            return total

        image = lax.fori_loop(0, n // 4, far_terms, image).reshape(clusters, rhs, panels)

        send_stats(1 + 2 * it, [row_sum(basis[b] * image) for b in range(it + 1)])
        inner = get_stats(1 + 2 * it, it + 1)
        rest = image
        for b in range(it + 1):
            rest = rest - inner[b][None] * basis[b]
        send_stats(2 + 2 * it, [row_sum(rest * rest)])
        (square,) = get_stats(2 + 2 * it, 1)
        norm = jnp.sqrt(square + epsilon)
        heights.extend(inner)
        heights.append(norm)
        following = rest / norm[None]
        if it == 0:
            basis[1] = following
        else:
            for c in range(clusters):
                out_ref[:, c * panels:(c + 1) * panels] = following[c]

    eye = lax.broadcasted_iota(jnp.int32, (rhs, rhs), 0) == lax.broadcasted_iota(jnp.int32, (rhs, rhs), 1)
    for place, height in enumerate(heights):
        hess_ref[place:place + 1, :] = jnp.sum(jnp.where(eye, height, 0.0), axis=0, keepdims=True)

    for index in range(REDUCTIONS):
        wait_bytes(stat_recv.at[index, pl.ds(0, n - 1)], stat_ssem.at[index])
    wait_bytes(factors.at[pl.ds(0, n - 1), pl.ds(0, used)], fact_ssem.at[0])
    wait_bytes(id_recv.at[pl.ds(0, n - 1)], id_ssem.at[0])
    for it in range(2):
        for side in range(2):
            wait_bytes(halo_send.at[it], halo_ssem.at[it, side])
            wait_bytes(part_send.at[it, side], part_ssem.at[it, side])
        wait_bytes(message_recv.at[it, pl.ds(0, n - 1)], msg_ssem.at[it])


def per_device(start, self_blocks, near_pairs, near_blocks, far_pairs, far_left, far_right):
    n = lax.axis_size("dev")
    me = lax.axis_index("dev")
    rhs, width = start.shape
    clusters, panels, _ = self_blocks.shape
    pairs = near_pairs.shape[1]
    far_count = far_pairs.shape[1]
    rank = far_left.shape[1]
    most = max(2, 2 * far_count // n)
    used = most * rank
    flat = clusters * rhs
    near_rows = near_pairs[0] - me * clusters
    near_cols = near_pairs[1] - (me - 1) * clusters
    near_ids = jnp.stack([near_rows, near_cols])
    keys = (near_ids[:, :, None] * rhs + jnp.arange(rhs, dtype=jnp.int32)).reshape(2, pairs * rhs)
    target = far_pairs[1] // clusters
    order = jnp.arange(far_count, dtype=jnp.int32)
    earlier = (target[:, None] == target[None, :]) & (order[None, :] < order[:, None])
    slot = target * most + jnp.sum(earlier.astype(jnp.int32), axis=1)
    hit = slot[None, :] == jnp.arange(n * most, dtype=jnp.int32)[:, None]
    code = order * (clusters * clusters) + (far_pairs[0] - me * clusters) * clusters + far_pairs[1] % clusters
    code = jnp.sum(jnp.where(hit, code[None, :] + 1, 0), axis=1) - 1
    filled = code >= 0
    perm = jnp.where(filled, code // (clusters * clusters), 0)

    def spread(ids):
        ids = jnp.where(filled, ids, -1).reshape(n, most, 1)
        ids = jnp.broadcast_to(ids, (n, most, rank)).reshape(n, 1, used)
        ids = jnp.pad(ids, ((0, 0), (0, 0), (0, LANES - used)), constant_values=-1)
        return jnp.broadcast_to(ids, (n, rhs, LANES))

    row_ids = spread(code // clusters % clusters)
    col_ids = spread(code % clusters)
    smem = pl.BlockSpec(memory_space=pltpu.SMEM)
    vmem = pl.BlockSpec(memory_space=pltpu.VMEM)
    hbm = pl.BlockSpec(memory_space=pl.ANY)
    dma = pltpu.SemaphoreType.DMA
    return pl.pallas_call(
        functools.partial(kernel, n, most, float(width * n)),
        out_shape=(
            jax.ShapeDtypeStruct((rhs, width), F32),
            jax.ShapeDtypeStruct((5, rhs), F32),
        ),
        in_specs=[smem, smem, vmem, vmem, vmem, vmem, hbm, hbm, hbm, hbm],
        out_specs=(vmem, vmem),
        scratch_shapes=[
            pltpu.VMEM(self_blocks.shape, BF16),
            pltpu.VMEM(near_blocks.shape, BF16),
            pltpu.VMEM(far_left.shape, BF16),
            pltpu.VMEM(far_right.shape, BF16),
            pltpu.VMEM((n, 2 * LANES, panels), BF16),
            pltpu.VMEM((n, used, panels), BF16),
            pltpu.VMEM((n, rhs, LANES), jnp.int32),
            pltpu.VMEM((REDUCTIONS, rhs, LANES), F32),
            pltpu.VMEM((REDUCTIONS, n, rhs, LANES), F32),
            pltpu.VMEM((2, flat, panels), BF16),
            pltpu.VMEM((2, 2, flat, panels), BF16),
            pltpu.VMEM((2, 2, flat, panels), BF16),
            pltpu.VMEM((2, 2, flat, panels), BF16),
            pltpu.VMEM((2, n, 2 * rhs, LANES), BF16),
            pltpu.VMEM((2, n, 2 * rhs, LANES), BF16),
            pltpu.VMEM((3 * clusters, rhs, panels), F32),
            pltpu.VMEM((pairs, rhs, panels), F32),
            pltpu.VMEM((2, clusters, rhs, panels), F32),
            dma((3 + NEAR_CHUNKS,)),
            dma((REDUCTIONS,)),
            dma((REDUCTIONS,)),
            dma((1,)), dma((1,)), dma((1,)), dma((1,)),
            dma((2, 2)), dma((2, 2)), dma((2, 2)), dma((2, 2)),
            dma((2,)), dma((2,)),
        ],
        compiler_params=pltpu.CompilerParams(
            collective_id=0, has_side_effects=True, vmem_limit_bytes=60 * 1024 * 1024
        ),
    )(near_ids, perm, start, keys, row_ids, col_ids, self_blocks, near_blocks, far_left, far_right)


def solution(mesh):
    in_specs = (
        P(None, "dev"),
        P("dev", None, None),
        P(None, "dev"),
        P("dev", None, None),
        P(None, "dev"),
        P("dev", None, None),
        P("dev", None, None),
    )
    out_specs = (P(None, "dev"), P())
    return jax.shard_map(
        per_device, mesh=mesh, in_specs=in_specs, out_specs=out_specs, check_vma=False
    )
```

time: 467 us -> 124 us (0.27)
  blocking collectives: 269 us -> 0 us
  Pallas kernels: 0 us -> 114 us
  waiting for transfers between devices: 59.7 us -> 0 us
  starting transfers between devices: 49.7 us -> 0 us
  matrix products: 43.6 us -> 0 us
  local copies, waits for them, and re-layouts: 33.7 us -> 4.72 us
    psum x6 -> x0, blocking collectives: 269 us -> none  [the longest x3 147 us: orthogonalize(): height = lax.psum(jnp.sum(vector * remainder, axis=1), 'dev') / count]
    pallas_call x0 -> x1, Pallas kernels: none -> 114 us  [per_device(): pl.pallas_call(functools.partial(kernel, n, most, float(width * n)), out_...]
    all_to_all x5 -> x0, waiting for transfers between devices: 57.8 us -> none  [the longest x2 33.1 us: apply_operator(): lax.all_to_all(served, 'dev', split_axis=0, concat_axis=0, tiled=True)]
    dot_general x18 -> x0, matrix products: 43.6 us -> none  [the longest x2 15.9 us: apply_operator(): jnp.einsum('prb,pab->pra', extended[near_cols], near_blocks, preferred_el...]
    ppermute x8 -> x0, starting transfers between devices: 25.1 us -> none  [the longest x4 18.4 us: from_behind(): lax.ppermute(value, axis, [(source, source + steps) for source in range(l...]
    all_to_all x5 -> x0, starting transfers between devices: 24.6 us -> none  [the longest x2 9.74 us: apply_operator(): lax.all_to_all(served, 'dev', split_axis=0, concat_axis=0, tiled=True)]
    gather x10 -> x0, local copies, waits for them, and re-layouts: 10.9 us -> none  [the longest x2 2.98 us: apply_operator(): local[row_local]]
    scatter x3 -> x0, local copies, waits for them, and re-layouts: 7.68 us -> none  [the longest x2 6.71 us: apply_operator(): outbox = jnp.zeros((devices * most, flat_width), jnp.float32).at[slot].se...]
  transfers between devices with their start and end apart: 13 -> 0, of which waited for: 5 -> 0; matrix products, arithmetic and copies ran while one was open for 15% -> 0% of each run, Pallas kernels for 0% -> 0%
where the time goes in v1:
time: 124 us
  Pallas kernels  114 us (92%)
  local copies, waits for them, and re-layouts  4.72 us (4%)
  other arithmetic  4.28 us (3%)
    pallas_call x1, Pallas kernels, per_device(): pl.pallas_call(functools.partial(kernel, n, most, float(width * n)), out_...  114 us
    unnamed x2, local copies, waits for them, and re-layouts  2.74 us

profile of v1, /device:TPU:0, one launch (start us, length us, event | category | flops | bytes accessed | tf_op | source)
XLA Modules:
  0.0 124.1 jit_solution(14498743129168617836)
XLA Ops:
  0.6 0.7 and_select_fusion.2
  1.3 0.8 slice_subtract_fusion.1
  2.1 0.8 and_select_fusion.3
  2.9 0.2 convert_reduce_fusion
  3.0 0.1 select_reduce_fusion
  3.2 0.6 broadcast_add_fusion.1
  3.7 0.6 broadcast_multiply_fusion
  4.3 0.1 sub.59
  4.4 0.1 copy.15
  4.5 0.1 copy.13
  4.5 0.1 add.94
  4.7 0.1 copy.14
  4.7 0.1 copy.16
  4.8 0.1 add.91
  4.9 0.1 add.92
  5.0 0.6 broadcast_add_fusion.keys_ref
  5.6 0.7 broadcast_in_dim.59.col_ids
  6.3 0.7 broadcast_in_dim.56.row_ids
  6.9 114.4 %shard_map.86 = (f32[8,2048]{1,0:T(8,128)}, f32[5,8]{1,0:T(8,128)}) custom-call(s32[2,96]{1,0:T(2,128)} %get-tuple-element.7.near_ids, s32[256]{0:T(256)} %get-tuple-element.5.perm, f32[8,2048]{1,0:T(8,128)} %start_ref.1, s32[2,768]{1,0:T(2,128)} %broadcast_add_fusion.keys_ref, s32[32,8,128]{2,1,0:T(8,128)} %broadcast_in_dim.56.row_ids, ...), custom_call_target="tpu_custom_call" | custom-call | tf_op jit(solution)/shard_map/pallas_call | solution.py:325
  121.3 1.5 %copy.19 = f32[8,2048]{1,0:T(8,128)} copy(f32[8,2048]{1,0:T(8,128)} %get-tuple-element.14) | data formatting | bytes 131072
  122.8 1.3 %copy.20 = f32[5,8]{1,0:T(8,128)} copy(f32[5,8]{1,0:T(8,128)} %get-tuple-element.15) | data formatting | bytes 320
  (5 shorter events, 0.1 us)

commit v2 on v1

--- a/solution.py
+++ b/solution.py
@@ -12,7 +12,10 @@
 F32 = jnp.float32
 BF16 = jnp.bfloat16
 NEAR_CHUNKS = 4
-REDUCTIONS = 5
+REDUCTIONS = 3
+STATS = 16
+STRIDE = 13
+TINY = 1e-20
 
 
 def dot_nn(a, b):
@@ -57,7 +60,7 @@
 
     def peer_loop(body):
         def step(i, carry):
-            body(lax.rem(me + i, n))
+            body(lax.rem(me + i * STRIDE, n))
             return carry
         lax.fori_loop(1, n, step, 0)
 
@@ -85,12 +88,20 @@
     barrier = pltpu.get_barrier_semaphore()
     peer_loop(lambda peer: pl.semaphore_signal(barrier, inc=1, device_id=(peer,), device_id_type=MESH))
 
-    lane = lax.broadcasted_iota(jnp.int32, (rhs, LANES), 1)
-
-    def send_stats(index, values):
-        block = jnp.zeros((rhs, LANES), F32)
-        for place, value in enumerate(values):
-            block = jnp.where(lane == place, value, block)
+    eye = lax.broadcasted_iota(jnp.int32, (rhs, LANES), 0) == lax.broadcasted_iota(
+        jnp.int32, (rhs, LANES), 1
+    )
+
+    def to_row(column):
+        return jnp.sum(jnp.where(eye, column, 0.0), axis=0, keepdims=True)
+
+    def to_column(row):
+        return jnp.sum(jnp.where(eye, row, 0.0), axis=1, keepdims=True)
+
+    def send_stats(index, columns):
+        rows = [to_row(column) for column in columns]
+        rows.append(jnp.zeros((STATS - len(rows), LANES), F32))
+        block = jnp.concatenate(rows, axis=0)
         stat_send[index] = block
         stat_recv[index, me] = block
         peer_loop(lambda peer: remote(
@@ -99,11 +110,10 @@
 
     def get_stats(index, count):
         wait_bytes(stat_recv.at[index, pl.ds(0, n - 1)], stat_rsem.at[index])
-        total = jnp.sum(stat_recv[index], axis=0)
-        return [
-            jnp.sum(jnp.where(lane == place, total, 0.0), axis=1, keepdims=True) / total_count
-            for place in range(count)
-        ]
+        return [stat_recv[index, :, place, :] for place in range(count)]
+
+    def mean(terms):
+        return jnp.sum(terms, axis=0, keepdims=True) / total_count
 
     first = jnp.stack([start_ref[:, c * panels:(c + 1) * panels] for c in range(clusters)], axis=0)
     partial = row_sum(first * first)
@@ -140,7 +150,7 @@
     peer_loop(send_factors)
 
     (square,) = get_stats(0, 1)
-    scale = jnp.sqrt(square + epsilon)
+    scale = to_column(jnp.sqrt(mean(square) + epsilon))
     basis[0] = first / scale[None]
 
     for load in loads:
@@ -253,26 +263,48 @@
 
         image = lax.fori_loop(0, n // 4, far_terms, image).reshape(clusters, rhs, panels)
 
-        send_stats(1 + 2 * it, [row_sum(basis[b] * image) for b in range(it + 1)])
-        inner = get_stats(1 + 2 * it, it + 1)
+        count = it + 1
+        vectors = [basis[b] for b in range(count)]
+        inner = [row_sum(v * image) for v in vectors]
+        gram = [row_sum(vectors[b] * vectors[d]) for b in range(count) for d in range(b, count)]
+        diagonal = [gram[0]] if it == 0 else [gram[0], gram[2]]
+        near_rest = image
+        guesses = []
+        for b in range(count):
+            product = inner[0] if b == 0 else row_sum(vectors[b] * near_rest)
+            wide = diagonal[b] > TINY
+            guess = jnp.where(wide, product / jnp.where(wide, diagonal[b], 1.0), 0.0)
+            near_rest = near_rest - guess[None] * vectors[b]
+            guesses.append(guess)
+        left_over = [row_sum(v * near_rest) for v in vectors]
+        columns = inner + guesses + left_over + gram + [row_sum(near_rest * near_rest)]
+        send_stats(1 + it, columns)
+        got = get_stats(1 + it, len(columns))
+        rows = [mean(got[b]) for b in range(count)]
+        change = [rows[b] - got[count + b] for b in range(count)]
+        square = got[-1]
+        for b in range(count):
+            square = square - 2.0 * change[b] * got[2 * count + b]
+        place = 3 * count
+        for b in range(count):
+            for d in range(b, count):
+                square = square + (1.0 if b == d else 2.0) * change[b] * change[d] * got[place]
+                place += 1
+        norm = jnp.sqrt(jnp.maximum(mean(square), 0.0) + epsilon)
         rest = image
-        for b in range(it + 1):
-            rest = rest - inner[b][None] * basis[b]
-        send_stats(2 + 2 * it, [row_sum(rest * rest)])
-        (square,) = get_stats(2 + 2 * it, 1)
-        norm = jnp.sqrt(square + epsilon)
-        heights.extend(inner)
+        for b in range(count):
+            rest = rest - to_column(rows[b])[None] * vectors[b]
+        heights.extend(rows)
         heights.append(norm)
-        following = rest / norm[None]
+        following = rest / to_column(norm)[None]
         if it == 0:
             basis[1] = following
         else:
             for c in range(clusters):
                 out_ref[:, c * panels:(c + 1) * panels] = following[c]
 
-    eye = lax.broadcasted_iota(jnp.int32, (rhs, rhs), 0) == lax.broadcasted_iota(jnp.int32, (rhs, rhs), 1)
     for place, height in enumerate(heights):
-        hess_ref[place:place + 1, :] = jnp.sum(jnp.where(eye, height, 0.0), axis=0, keepdims=True)
+        hess_ref[place:place + 1, :] = height[:, :rhs]
 
     for index in range(REDUCTIONS):
         wait_bytes(stat_recv.at[index, pl.ds(0, n - 1)], stat_ssem.at[index])
@@ -338,8 +370,8 @@
             pltpu.VMEM((n, 2 * LANES, panels), BF16),
             pltpu.VMEM((n, used, panels), BF16),
             pltpu.VMEM((n, rhs, LANES), jnp.int32),
-            pltpu.VMEM((REDUCTIONS, rhs, LANES), F32),
-            pltpu.VMEM((REDUCTIONS, n, rhs, LANES), F32),
+            pltpu.VMEM((REDUCTIONS, STATS, LANES), F32),
+            pltpu.VMEM((REDUCTIONS, n, STATS, LANES), F32),
             pltpu.VMEM((2, flat, panels), BF16),
             pltpu.VMEM((2, 2, flat, panels), BF16),
             pltpu.VMEM((2, 2, flat, panels), BF16),

time: 124 us -> 117 us (0.944)
  Pallas kernels: 114 us -> 107 us
    pallas_call x1, Pallas kernels: 114 us -> 107 us  [per_device(): pl.pallas_call(functools.partial(kernel, n, most, float(width * n)), out_...]
where the time goes in v2:
time: 117 us
  Pallas kernels  107 us (91%)
  local copies, waits for them, and re-layouts  4.72 us (4%)
  other arithmetic  4.28 us (4%)
    pallas_call x1, Pallas kernels, per_device(): pl.pallas_call(functools.partial(kernel, n, most, float(width * n)), out_...  107 us
    unnamed x2, local copies, waits for them, and re-layouts  2.74 us

profile of v2, /device:TPU:0, one launch (start us, length us, event | category | flops | bytes accessed | tf_op | source)
XLA Modules:
  0.0 117.0 jit_solution(9817621786462655869)
XLA Ops:
  0.6 0.7 and_select_fusion.2
  1.3 0.8 slice_subtract_fusion.1
  2.1 0.8 and_select_fusion.3
  2.9 0.2 convert_reduce_fusion
  3.0 0.1 select_reduce_fusion
  3.2 0.6 broadcast_add_fusion.1
  3.7 0.6 broadcast_multiply_fusion
  4.3 0.1 sub.59
  4.4 0.1 copy.15
  4.5 0.1 copy.13
  4.5 0.1 add.94
  4.7 0.1 copy.14
  4.7 0.1 copy.16
  4.8 0.1 add.91
  4.9 0.1 add.92
  5.0 0.6 broadcast_add_fusion.keys_ref
  5.6 0.7 broadcast_in_dim.59.col_ids
  6.3 0.7 broadcast_in_dim.56.row_ids
  6.9 107.3 %shard_map.86 = (f32[8,2048]{1,0:T(8,128)}, f32[5,8]{1,0:T(8,128)}) custom-call(s32[2,96]{1,0:T(2,128)} %get-tuple-element.7.near_ids, s32[256]{0:T(256)} %get-tuple-element.5.perm, f32[8,2048]{1,0:T(8,128)} %start_ref.1, s32[2,768]{1,0:T(2,128)} %broadcast_add_fusion.keys_ref, s32[32,8,128]{2,1,0:T(8,128)} %broadcast_in_dim.56.row_ids, ...), custom_call_target="tpu_custom_call" | custom-call | tf_op jit(solution)/shard_map/pallas_call | solution.py:357
  114.2 1.5 %copy.19 = f32[8,2048]{1,0:T(8,128)} copy(f32[8,2048]{1,0:T(8,128)} %get-tuple-element.14) | data formatting | bytes 131072
  115.7 1.3 %copy.20 = f32[5,8]{1,0:T(8,128)} copy(f32[5,8]{1,0:T(8,128)} %get-tuple-element.15) | data formatting | bytes 320
  (5 shorter events, 0.1 us)

commit v3 on v2

--- a/solution.py
+++ b/solution.py
@@ -43,9 +43,9 @@
     near_ids, perm, start_ref, keys_ref, row_ids, col_ids, self_hbm, near_hbm, left_hbm, right_hbm,
     out_ref, hess_ref,
     selfs, nears, lefts, rights, factors, outgoing, id_recv, stat_send, stat_recv,
-    halo_send, halo_recv, part_send, part_recv, message, message_recv,
+    raw_recv, halo_send, halo_recv, part_send, part_recv, message, message_recv,
     extended, terms, basis,
-    load_sem, stat_ssem, stat_rsem, fact_ssem, fact_rsem, id_ssem, id_rsem,
+    load_sem, raw_ssem, raw_rsem, stat_ssem, stat_rsem, fact_ssem, fact_rsem, id_ssem, id_rsem,
     halo_ssem, halo_rsem, part_ssem, part_rsem, msg_ssem, msg_rsem,
 ):
     me = lax.axis_index("dev")
@@ -58,11 +58,11 @@
     used = most * rank
     flat = clusters * rhs
 
-    def peer_loop(body):
+    def peer_loop(body, unroll=True):
         def step(i, carry):
             body(lax.rem(me + i * STRIDE, n))
             return carry
-        lax.fori_loop(1, n, step, 0)
+        lax.fori_loop(1, n, step, 0, unroll=unroll and n <= 32)
 
     def remote(src, dst, ssem, rsem, peer):
         return pltpu.make_async_remote_copy(
@@ -131,6 +131,12 @@
 
     pl.semaphore_wait(barrier, n - 1)
     send_stats(0, [partial])
+    raws = [
+        remote(start_ref, raw_recv.at[0], raw_ssem.at[0], raw_rsem.at[0], after),
+        remote(start_ref, raw_recv.at[1], raw_ssem.at[1], raw_rsem.at[1], before),
+    ]
+    for raw in raws:
+        raw.start()
 
     right_copy.wait()
     left_copy.wait()
@@ -143,11 +149,15 @@
         remote(
             outgoing.at[peer], factors.at[me, pl.ds(0, used)], fact_ssem.at[0], fact_rsem.at[0], peer
         ).start()
+
+    peer_loop(send_factors, False)
+
+    def place_left(peer):
         for m in range(most):
             pair = perm[peer * most + m]
             factors[peer, pl.ds(LANES + m * rank, rank)] = lefts[pair]
 
-    peer_loop(send_factors)
+    peer_loop(place_left, False)
 
     (square,) = get_stats(0, 1)
     scale = to_column(jnp.sqrt(mean(square) + epsilon))
@@ -159,13 +169,16 @@
     heights = []
     for it in range(2):
         vector = basis[it].reshape(flat, panels).astype(BF16)
-        halo_send[it] = vector
-        halos = [
-            remote(halo_send.at[it], halo_recv.at[it, 0], halo_ssem.at[it, 0], halo_rsem.at[it, 0], after),
-            remote(halo_send.at[it], halo_recv.at[it, 1], halo_ssem.at[it, 1], halo_rsem.at[it, 1], before),
-        ]
-        for halo in halos:
-            halo.start()
+        if it == 0:
+            halos = raws
+        else:
+            halo_send[...] = vector
+            halos = [
+                remote(halo_send, halo_recv.at[0], halo_ssem.at[0], halo_rsem.at[0], after),
+                remote(halo_send, halo_recv.at[1], halo_ssem.at[1], halo_rsem.at[1], before),
+            ]
+            for halo in halos:
+                halo.start()
         extended[pl.ds(clusters, clusters)] = vector.astype(F32).reshape(clusters, rhs, panels)
 
         def exchange_far():
@@ -173,9 +186,9 @@
                 wait_bytes(factors.at[pl.ds(0, n - 1), pl.ds(0, used)], fact_rsem.at[0])
                 wait_bytes(id_recv.at[pl.ds(0, n - 1)], id_rsem.at[0])
 
-            def products(t4, carry):
-                for u in range(4):
-                    t = t4 * 4 + u
+            def products(t8, carry):
+                for u in range(8):
+                    t = t8 * 8 + u
                     e = dot_nt(vector, factors[t])
                     coeff = jnp.zeros((rhs, LANES), F32)
                     lean = jnp.zeros((rhs, LANES), F32)
@@ -186,7 +199,7 @@
                     message[it, t] = jnp.concatenate([coeff, lean], axis=0).astype(BF16)
                 return carry
 
-            lax.fori_loop(0, n // 4, products, 0)
+            lax.fori_loop(0, n // 8, products, 0)
             peer_loop(lambda peer: remote(
                 message.at[it, peer], message_recv.at[it, me], msg_ssem.at[it], msg_rsem.at[it], peer
             ).start())
@@ -195,13 +208,13 @@
             exchange_far()
 
         def to_cols(p8, carry):
-            for u in range(8):
-                p = p8 * 8 + u
+            for u in range(16):
+                p = p8 * 16 + u
                 x = extended[near_ids[0, p] + clusters].astype(BF16)
                 terms[p] = dot_nn(x, nears[p])
             return carry
 
-        lax.fori_loop(0, pairs // 8, to_cols, 0)
+        lax.fori_loop(0, pairs // 16, to_cols, 0)
         sums = one_hot_sum(keys_ref[1:2, :], terms[...].reshape(pairs * rhs, panels), 3 * flat)
         part_send[it, 0] = sums[:flat].astype(BF16)
         part_send[it, 1] = sums[2 * flat:].astype(BF16)
@@ -217,19 +230,24 @@
         )
         for halo in halos:
             halo.wait_recv()
-        extended[pl.ds(0, clusters)] = halo_recv[it, 0].astype(F32).reshape(clusters, rhs, panels)
-        extended[pl.ds(2 * clusters, clusters)] = halo_recv[it, 1].astype(F32).reshape(
-            clusters, rhs, panels
-        )
+        for side in range(2):
+            if it == 0:
+                for c in range(clusters):
+                    raw = raw_recv[side, :, c * panels:(c + 1) * panels]
+                    extended[2 * clusters * side + c] = raw / scale
+            else:
+                extended[pl.ds(2 * clusters * side, clusters)] = halo_recv[side].astype(F32).reshape(
+                    clusters, rhs, panels
+                )
 
         def to_rows(p8, carry):
-            for u in range(8):
-                p = p8 * 8 + u
+            for u in range(16):
+                p = p8 * 16 + u
                 x = extended[near_ids[1, p]].astype(BF16)
                 terms[p] = dot_nt(x, nears[p])
             return carry
 
-        lax.fori_loop(0, pairs // 8, to_rows, 0)
+        lax.fori_loop(0, pairs // 16, to_rows, 0)
         image = image + one_hot_sum(keys_ref[0:1, :], terms[...].reshape(pairs * rhs, panels), flat)
         if it == 0:
             exchange_far()
@@ -240,9 +258,9 @@
         image = image + part_recv[it, 0].astype(F32) * has_after + part_recv[it, 1].astype(F32) * has_before
         wait_bytes(message_recv.at[it, pl.ds(0, n - 1)], msg_rsem.at[it])
 
-        def far_terms(t4, total):
-            for u in range(4):
-                t = t4 * 4 + u
+        def far_terms(t8, total):
+            for u in range(8):
+                t = t8 * 8 + u
                 arrived = message_recv[it, t].astype(F32)
                 coeff, lean = arrived[:rhs], arrived[rhs:]
                 spread = jnp.concatenate(
@@ -261,7 +279,7 @@
                 total = total + dot_nn(spread, factors[t])
             return total
 
-        image = lax.fori_loop(0, n // 4, far_terms, image).reshape(clusters, rhs, panels)
+        image = lax.fori_loop(0, n // 8, far_terms, image).reshape(clusters, rhs, panels)
 
         count = it + 1
         vectors = [basis[b] for b in range(count)]
@@ -310,9 +328,11 @@
         wait_bytes(stat_recv.at[index, pl.ds(0, n - 1)], stat_ssem.at[index])
     wait_bytes(factors.at[pl.ds(0, n - 1), pl.ds(0, used)], fact_ssem.at[0])
     wait_bytes(id_recv.at[pl.ds(0, n - 1)], id_ssem.at[0])
+    for side in range(2):
+        wait_bytes(start_ref, raw_ssem.at[side])
+        wait_bytes(halo_send, halo_ssem.at[side])
     for it in range(2):
         for side in range(2):
-            wait_bytes(halo_send.at[it], halo_ssem.at[it, side])
             wait_bytes(part_send.at[it, side], part_ssem.at[it, side])
         wait_bytes(message_recv.at[it, pl.ds(0, n - 1)], msg_ssem.at[it])
 
@@ -372,8 +392,9 @@
             pltpu.VMEM((n, rhs, LANES), jnp.int32),
             pltpu.VMEM((REDUCTIONS, STATS, LANES), F32),
             pltpu.VMEM((REDUCTIONS, n, STATS, LANES), F32),
+            pltpu.VMEM((2, rhs, width), F32),
+            pltpu.VMEM((flat, panels), BF16),
             pltpu.VMEM((2, flat, panels), BF16),
-            pltpu.VMEM((2, 2, flat, panels), BF16),
             pltpu.VMEM((2, 2, flat, panels), BF16),
             pltpu.VMEM((2, 2, flat, panels), BF16),
             pltpu.VMEM((2, n, 2 * rhs, LANES), BF16),
@@ -382,10 +403,11 @@
             pltpu.VMEM((pairs, rhs, panels), F32),
             pltpu.VMEM((2, clusters, rhs, panels), F32),
             dma((3 + NEAR_CHUNKS,)),
+            dma((2,)), dma((2,)),
             dma((REDUCTIONS,)),
             dma((REDUCTIONS,)),
             dma((1,)), dma((1,)), dma((1,)), dma((1,)),
-            dma((2, 2)), dma((2, 2)), dma((2, 2)), dma((2, 2)),
+            dma((2,)), dma((2,)), dma((2, 2)), dma((2, 2)),
             dma((2,)), dma((2,)),
         ],
         compiler_params=pltpu.CompilerParams(

time: 117 us -> 110 us (0.940)
  Pallas kernels: 107 us -> 100 us
    pallas_call x1, Pallas kernels: 107 us -> 100 us  [per_device(): pl.pallas_call(functools.partial(kernel, n, most, float(width * n)), out_...]
where the time goes in v3:
time: 110 us
  Pallas kernels  100 us (91%)
  local copies, waits for them, and re-layouts  4.72 us (4%)
  other arithmetic  4.28 us (4%)
    pallas_call x1, Pallas kernels, per_device(): pl.pallas_call(functools.partial(kernel, n, most, float(width * n)), out_...  100 us
    unnamed x2, local copies, waits for them, and re-layouts  2.74 us

profile of v3, /device:TPU:0, one launch (start us, length us, event | category | flops | bytes accessed | tf_op | source)
XLA Modules:
  0.0 110.1 jit_solution(4117190174884012445)
XLA Ops:
  0.6 0.7 and_select_fusion.2
  1.3 0.8 slice_subtract_fusion.1
  2.1 0.8 and_select_fusion.3
  2.9 0.2 convert_reduce_fusion
  3.0 0.1 select_reduce_fusion
  3.2 0.6 broadcast_add_fusion.1
  3.7 0.6 broadcast_multiply_fusion
  4.3 0.1 sub.59
  4.4 0.1 copy.15
  4.5 0.1 copy.13
  4.5 0.1 add.94
  4.7 0.1 copy.14
  4.7 0.1 copy.16
  4.8 0.1 add.91
  4.9 0.1 add.92
  5.0 0.6 broadcast_add_fusion.keys_ref
  5.6 0.7 broadcast_in_dim.59.col_ids
  6.3 0.7 broadcast_in_dim.56.row_ids
  6.9 100.4 %shard_map.86 = (f32[8,2048]{1,0:T(8,128)}, f32[5,8]{1,0:T(8,128)}) custom-call(s32[2,96]{1,0:T(2,128)} %get-tuple-element.7.near_ids, s32[256]{0:T(256)} %get-tuple-element.5.perm, f32[8,2048]{1,0:T(8,128)} %start_ref.1, s32[2,768]{1,0:T(2,128)} %broadcast_add_fusion.keys_ref, s32[32,8,128]{2,1,0:T(8,128)} %broadcast_in_dim.56.row_ids, ...), custom_call_target="tpu_custom_call" | custom-call | tf_op jit(solution)/shard_map/pallas_call | solution.py:377
  107.4 1.5 %copy.19 = f32[8,2048]{1,0:T(8,128)} copy(f32[8,2048]{1,0:T(8,128)} %get-tuple-element.14) | data formatting | bytes 131072
  108.8 1.3 %copy.20 = f32[5,8]{1,0:T(8,128)} copy(f32[5,8]{1,0:T(8,128)} %get-tuple-element.15) | data formatting | bytes 320
  (5 shorter events, 0.1 us)

commit v4 on v3

--- a/solution.py
+++ b/solution.py
@@ -187,8 +187,8 @@
                 wait_bytes(id_recv.at[pl.ds(0, n - 1)], id_rsem.at[0])
 
             def products(t8, carry):
-                for u in range(8):
-                    t = t8 * 8 + u
+                for u in range(16):
+                    t = t8 * 16 + u
                     e = dot_nt(vector, factors[t])
                     coeff = jnp.zeros((rhs, LANES), F32)
                     lean = jnp.zeros((rhs, LANES), F32)
@@ -199,7 +199,7 @@
                     message[it, t] = jnp.concatenate([coeff, lean], axis=0).astype(BF16)
                 return carry
 
-            lax.fori_loop(0, n // 8, products, 0)
+            lax.fori_loop(0, n // 16, products, 0)
             peer_loop(lambda peer: remote(
                 message.at[it, peer], message_recv.at[it, me], msg_ssem.at[it], msg_rsem.at[it], peer
             ).start())
@@ -208,13 +208,13 @@
             exchange_far()
 
         def to_cols(p8, carry):
-            for u in range(16):
-                p = p8 * 16 + u
+            for u in range(32):
+                p = p8 * 32 + u
                 x = extended[near_ids[0, p] + clusters].astype(BF16)
                 terms[p] = dot_nn(x, nears[p])
             return carry
 
-        lax.fori_loop(0, pairs // 16, to_cols, 0)
+        lax.fori_loop(0, pairs // 32, to_cols, 0)
         sums = one_hot_sum(keys_ref[1:2, :], terms[...].reshape(pairs * rhs, panels), 3 * flat)
         part_send[it, 0] = sums[:flat].astype(BF16)
         part_send[it, 1] = sums[2 * flat:].astype(BF16)
@@ -241,13 +241,13 @@
                 )
 
         def to_rows(p8, carry):
-            for u in range(16):
-                p = p8 * 16 + u
+            for u in range(32):
+                p = p8 * 32 + u
                 x = extended[near_ids[1, p]].astype(BF16)
                 terms[p] = dot_nt(x, nears[p])
             return carry
 
-        lax.fori_loop(0, pairs // 16, to_rows, 0)
+        lax.fori_loop(0, pairs // 32, to_rows, 0)
         image = image + one_hot_sum(keys_ref[0:1, :], terms[...].reshape(pairs * rhs, panels), flat)
         if it == 0:
             exchange_far()
@@ -259,8 +259,8 @@
         wait_bytes(message_recv.at[it, pl.ds(0, n - 1)], msg_rsem.at[it])
 
         def far_terms(t8, total):
-            for u in range(8):
-                t = t8 * 8 + u
+            for u in range(16):
+                t = t8 * 16 + u
                 arrived = message_recv[it, t].astype(F32)
                 coeff, lean = arrived[:rhs], arrived[rhs:]
                 spread = jnp.concatenate(
@@ -279,7 +279,7 @@
                 total = total + dot_nn(spread, factors[t])
             return total
 
-        image = lax.fori_loop(0, n // 8, far_terms, image).reshape(clusters, rhs, panels)
+        image = lax.fori_loop(0, n // 16, far_terms, image).reshape(clusters, rhs, panels)
 
         count = it + 1
         vectors = [basis[b] for b in range(count)]

time: 110 us -> 109 us (level)
  Pallas kernels: 100 us -> 98.7 us
    pallas_call x1, Pallas kernels: 100 us -> 98.7 us  [per_device(): pl.pallas_call(functools.partial(kernel, n, most, float(width * n)), out_...]
where the time goes in v4:
time: 109 us; the launch traced here: 108 us
  Pallas kernels  98.7 us (91%)
  local copies, waits for them, and re-layouts  4.72 us (4%)
  other arithmetic  4.28 us (4%)
    pallas_call x1, Pallas kernels, per_device(): pl.pallas_call(functools.partial(kernel, n, most, float(width * n)), out_...  98.7 us
    unnamed x2, local copies, waits for them, and re-layouts  2.74 us

profile of v4, /device:TPU:0, one launch (start us, length us, event | category | flops | bytes accessed | tf_op | source)
XLA Modules:
  0.0 108.4 jit_solution(15025837623368491364)
XLA Ops:
  0.6 0.7 and_select_fusion.2
  1.3 0.8 slice_subtract_fusion.1
  2.1 0.8 and_select_fusion.3
  2.9 0.2 convert_reduce_fusion
  3.0 0.1 select_reduce_fusion
  3.2 0.6 broadcast_add_fusion.1
  3.7 0.6 broadcast_multiply_fusion
  4.3 0.1 sub.59
  4.4 0.1 copy.15
  4.5 0.1 copy.13
  4.5 0.1 add.94
  4.7 0.1 copy.14
  4.7 0.1 copy.16
  4.8 0.1 add.91
  4.9 0.1 add.92
  5.0 0.6 broadcast_add_fusion.keys_ref
  5.6 0.7 broadcast_in_dim.59.col_ids
  6.3 0.7 broadcast_in_dim.56.row_ids
  6.9 98.7 %shard_map.86 = (f32[8,2048]{1,0:T(8,128)}, f32[5,8]{1,0:T(8,128)}) custom-call(s32[2,96]{1,0:T(2,128)} %get-tuple-element.7.near_ids, s32[256]{0:T(256)} %get-tuple-element.5.perm, f32[8,2048]{1,0:T(8,128)} %start_ref.1, s32[2,768]{1,0:T(2,128)} %broadcast_add_fusion.keys_ref, s32[32,8,128]{2,1,0:T(8,128)} %broadcast_in_dim.56.row_ids, ...), custom_call_target="tpu_custom_call" | custom-call | tf_op jit(solution)/shard_map/pallas_call | solution.py:377
  105.7 1.5 %copy.19 = f32[8,2048]{1,0:T(8,128)} copy(f32[8,2048]{1,0:T(8,128)} %get-tuple-element.14) | data formatting | bytes 131072
  107.1 1.3 %copy.20 = f32[5,8]{1,0:T(8,128)} copy(f32[5,8]{1,0:T(8,128)} %get-tuple-element.15) | data formatting | bytes 320
  (5 shorter events, 0.1 us)
